TPU v7x, 128 devices: a whole 4x4x4 slice. The times are simulated.
128 devices in a mesh: row: 16 (over y, x_hi, core), col: 8 (over z, x_lo).
Axes of the slice: x: 4 (x_hi: 2, x_lo: 2; x = x_hi * 2 + x_lo), y: 4, z: 4, core: 2. Of those that a mesh axis runs over, the one named last changes fastest.
Arguments:
- homolog_embedding: bfloat16 [1024, 1024, 256], P(('row', 'col')), may hold values from -6 to 6
- presence_indicator: int32 [1024, 1024], P(('row', 'col')), may hold values 0 or 1
- standardizer_multiplier: float32 [256], replicated, may hold values from 0.5 to 1.5
- standardizer_offset: float32 [256], replicated, may hold values from -1.5 to 1.5
- first_factor_matrix: bfloat16 [256, 32], replicated, may hold values from -0.375 to 0.375
- first_factor_offset: float32 [32], replicated, may hold values from -1.5 to 1.5
- second_factor_matrix: bfloat16 [256, 32], replicated, may hold values from -0.375 to 0.375
- second_factor_offset: float32 [32], replicated, may hold values from -1.5 to 1.5
- final_matrix: bfloat16 [1024, 128], replicated, may hold values from -0.59765625 to 0.59765625
- final_offset: float32 [128], replicated, may hold values from -1.5 to 1.5
Outputs:
- pair_update: bfloat16 [1024, 1024, 128], P('row', 'col')
All inputs are finite; a program needn't handle non-finite values. No bound on the sum of `presence_indicator` on one device may be relied on, other than what follows from the above.
Results may differ from a plain program's by a relative error of at most 0.0052.
Values may be sent and summed in bfloat16 or wider, within the bound.
A program may use at most 320 MiB of HBM per device.

v0:
```python
import jax
import jax.numpy as jnp
from jax import lax
from jax.sharding import PartitionSpec as P


def standardize_features(homolog_embedding, standardizer_multiplier, standardizer_offset):
    input_tensor = homolog_embedding.astype(jnp.float32)
    center = jnp.mean(input_tensor, axis=-1, keepdims=True)
    spread = jnp.mean((input_tensor - center) ** 2, axis=-1, keepdims=True)
    return (
        (input_tensor - center) * lax.rsqrt(spread + 1e-05) * standardizer_multiplier
        + standardizer_offset
    ).astype(jnp.bfloat16)


def linear_map(standardized_embedding, expanded_indicator, coefficient_matrix, additive_offset):
    reshaped_matrix = standardized_embedding.reshape(-1, standardized_embedding.shape[-1])
    input_tensor = jnp.dot(
        reshaped_matrix, coefficient_matrix, preferred_element_type=jnp.float32
    ).reshape(standardized_embedding.shape[:-1] + (coefficient_matrix.shape[1],))
    return (
        expanded_indicator.astype(jnp.float32)[..., None] * (input_tensor + additive_offset)
    ).astype(jnp.bfloat16)


def finish_tile(outer_rows, count_rows, weight3, final_offset, block, width, cols_here):
    outer_rows = outer_rows.reshape(block, width, cols_here, width)
    mean = (outer_rows / (count_rows[:, None, :, None] + 0.001)).astype(jnp.bfloat16)
    update = (
        jnp.einsum("icje,ceh->ijh", mean, weight3, preferred_element_type=jnp.float32)
        + final_offset
    )
    return update.astype(jnp.bfloat16)


def shards(
    homolog_embedding,
    presence_indicator,
    standardizer_multiplier,
    standardizer_offset,
    first_factor_matrix,
    first_factor_offset,
    second_factor_matrix,
    second_factor_offset,
    final_matrix,
    final_offset,
):
    expanded_indicator = presence_indicator.astype(jnp.bfloat16)
    standardized_embedding = standardize_features(
        homolog_embedding, standardizer_multiplier, standardizer_offset
    )
    transmit_first = linear_map(
        standardized_embedding, expanded_indicator, first_factor_matrix, first_factor_offset
    )
    transmit_second = linear_map(
        standardized_embedding, expanded_indicator, second_factor_matrix, second_factor_offset
    )
    left_part, left_mpart = (
        lax.all_to_all(transmit_first, "row", split_axis=1, concat_axis=0, tiled=True),
        lax.all_to_all(expanded_indicator, "row", split_axis=1, concat_axis=0, tiled=True),
    )
    left_all, left_mask = (
        lax.all_gather(left_part, "col", axis=0, tiled=True),
        lax.all_gather(left_mpart, "col", axis=0, tiled=True),
    )
    right_part, right_mpart = (
        lax.all_to_all(transmit_second, "col", split_axis=1, concat_axis=0, tiled=True),
        lax.all_to_all(expanded_indicator, "col", split_axis=1, concat_axis=0, tiled=True),
    )
    n_row = lax.axis_size("row")
    n_col = lax.axis_size("col")
    seqs = left_all.shape[0]
    rows_here = left_all.shape[1]
    cols_here = right_part.shape[1]
    left_all = left_all.reshape((n_col, n_row, seqs // (n_row * n_col)) + left_all.shape[1:])
    left_all = jnp.swapaxes(left_all, 0, 1).reshape((seqs,) + left_all.shape[3:])
    left_mask = left_mask.reshape(n_col, n_row, seqs // (n_row * n_col), rows_here)
    left_mask = jnp.swapaxes(left_mask, 0, 1).reshape(seqs, rows_here)
    width = left_all.shape[2]
    depth = final_matrix.shape[1]
    block = 16
    nblocks = rows_here // block
    weight3 = final_matrix.reshape(width, width, depth)
    right_all, right_mask = (
        lax.all_gather(right_part, "row", axis=0, tiled=True),
        lax.all_gather(right_mpart, "row", axis=0, tiled=True),
    )
    count = jnp.dot(left_mask.T, right_mask, preferred_element_type=jnp.float32)
    right_flat = right_all.reshape(seqs, cols_here * width)
    left_blocks = left_all.reshape(seqs, nblocks, block, width).transpose(1, 0, 2, 3)
    count_blocks = count.reshape(nblocks, block, cols_here)

    def one_block(item):
        left_blk, count_blk = item
        outer = lax.dot_general(
            left_blk.reshape(seqs, block * width),
            right_flat,
            (((0,), (0,)), ((), ())),
            preferred_element_type=jnp.float32,
        )
        return finish_tile(outer, count_blk, weight3, final_offset, block, width, cols_here)

    result = lax.map(one_block, (left_blocks, count_blocks))
    return result.reshape(rows_here, cols_here, depth)


def solution(mesh):
    in_specs = (
        P(("row", "col"), None, None),
        P(("row", "col"), None),
        P(),
        P(),
        P(),
        P(),
        P(),
        P(),
        P(),
        P(),
    )
    out_specs = P("row", "col", None)
    return jax.shard_map(shards, mesh=mesh, in_specs=in_specs, out_specs=out_specs, check_vma=False)
```

profile of v0, /device:TPU:1, one launch (start us, length us, event | category | flops | bytes accessed | tf_op | source)
XLA Modules:
  0.0 318.9 jit_solution(18399425859830764476)
XLA Ops:
  6.5 0.0 copy-start
  6.5 0.0 all-gather.3.cloned.1.call-start
  6.6 0.0 copy-start.2
  6.6 3.5 %convert_reduce_fusion = f32[8,1024]{1,0:T(8,128)S(1)} fusion(bf16[8,1024,256]{2,1,0:T(8,128)(2,1)} %param.12), kind=kLoop, calls=%fused_computation.16 | loop fusion | flops 4186112 | bytes 4227072 | tf_op jit(solution)/shard_map/reduce_sum | solution.py:9
  10.1 4.0 %fusion.15 = f32[8,1024]{1,0:T(8,128)S(1)} fusion(bf16[8,1024,256]{2,1,0:T(8,128)(2,1)} %param.12, f32[8,1024]{1,0:T(8,128)S(1)} %broadcast_multiply_fusion), kind=kLoop, calls=%fused_computation.19 | loop fusion | flops 8380416 | bytes 4259840 | tf_op jit(solution)/shard_map/reduce_sum | solution.py:10
  14.1 0.0 copy-done.4
  14.1 0.6 fusion.45
  14.7 0.0 copy-done
  14.8 0.0 copy-done.7
  14.8 0.0 copy-done.6
  14.8 0.0 copy-done.8
  14.8 0.0 copy-done.2
  14.8 3.8 %fusion.38 = bf16[8,1024,32]{1,2,0:T(8,128)(2,1)S(1)} fusion(bf16[8,1024,256]{2,1,0:T(8,128)(2,1)S(1)} %copy-done.2, f32[256]{0:T(256)S(1)} %copy-done.6, f32[256]{0:T(256)S(1)} %copy-done.7, f32[8,1024]{1,0:T(8,128)S(1)} %add_rsqrt_fusion, f32[8,1024]{1,0:T(8,128)S(1)} %broadcast_multiply_fusion, f32[32]{0:T(128)S(1)} %copy-done.8, ...), kind=kOutput, calls=%fused_computation.30 | convolution fusion | flops 147587072 | bytes 4835456 | tf_op jit(solution)/shard_map/dot_general | solution.py:19
  18.6 0.0 copy-start.5
  18.6 0.0 copy-start.9
  18.6 1.6 copy.46
  20.3 2.0 reshape.82
  22.3 19.5 %all_to_all.74 = bf16[16,2,8192]{2,1,0:T(2,128)(2,1)S(1)} all-to-all(bf16[16,2,8192]{2,1,0:T(2,128)(2,1)S(1)} %reshape.82), channel_id=1, replica_groups=mesh['row'=16,'col'=8] {'row'}, dimensions={0} | all-to-all | bytes 1048576 | tf_op jit(solution)/shard_map/all_to_all | solution.py:60
  41.8 1.0 reshape.83
  42.8 1.2 copy.47
  44.0 2.4 copy.48
  46.4 0.0 all-gather.3.cloned.1.call-update
  46.4 0.0 all-gather.5.cloned.1.call-start
  46.5 0.0 copy-done.5
  46.5 0.0 copy-done.9
  46.5 4.2 %fusion.35 = bf16[8,1024,32]{1,2,0:T(8,128)(2,1)S(1)} fusion(bf16[8,1024,256]{2,1,0:T(8,128)(2,1)} %param.12, f32[256]{0:T(256)S(1)} %copy-done.6, f32[256]{0:T(256)S(1)} %copy-done.7, f32[8,1024]{1,0:T(8,128)S(1)} %add_rsqrt_fusion, f32[8,1024]{1,0:T(8,128)S(1)} %broadcast_multiply_fusion, f32[32]{0:T(128)S(1)} %copy-done.9, ...), kind=kOutput, calls=%fused_computation.29 | convolution fusion | flops 147587072 | bytes 4835456 | tf_op jit(solution)/shard_map/dot_general | solution.py:19
  50.7 0.0 copy-start.3
  50.7 1.6 copy.51
  52.4 2.0 reshape.84
  54.4 20.6 %all_to_all.75 = bf16[8,2,16384]{2,1,0:T(2,128)(2,1)S(1)} all-to-all(bf16[8,2,16384]{2,1,0:T(2,128)(2,1)S(1)} %reshape.84), channel_id=1, replica_groups=mesh['row'=16,'col'=8] {'col'}, dimensions={0} | all-to-all | bytes 1048576 | tf_op jit(solution)/shard_map/all_to_all | solution.py:68
  74.9 1.0 reshape.85
  76.0 1.8 copy.53
  77.7 0.0 all-gather.5.cloned.1.call-update
  77.7 3.3 %all-to-all-start.3 = ((bf16[8,8,128]{2,0,1:T(8,128)(2,1)}), bf16[8,8,128]{2,0,1:T(8,128)(2,1)S(1)}, u32[]{:S(2)}, u32[]{:S(2)}) async-start(bf16[8,8,128]{2,0,1:T(8,128)(2,1)} %bitcast.34), calls=%async_computation.3 | async-start | bytes 32768 | tf_op jit(solution)/shard_map/all_to_all | solution.py:69
  81.0 0.8 all_to_all.62
  81.9 0.7 reshape.86
  82.6 0.0 copy-done.3
  82.6 0.1 copy.59
  82.7 3.4 %all-to-all-done.3 = bf16[8,8,128]{2,0,1:T(8,128)(2,1)S(1)} async-done(((bf16[8,8,128]{2,0,1:T(8,128)(2,1)}), bf16[8,8,128]{2,0,1:T(8,128)(2,1)S(1)}, u32[]{:S(2)}, u32[]{:S(2)}) %all-to-all-start.3) | async-done | bytes 16416 | tf_op jit(solution)/shard_map/all_to_all | solution.py:69
  86.1 6.6 %all-to-all-start.2 = ((bf16[16,2,256]{2,1,0:T(2,128)(2,1)}), bf16[16,2,256]{2,1,0:T(2,128)(2,1)S(1)}, u32[]{:S(2)}, u32[]{:S(2)}) async-start(bf16[16,2,256]{2,1,0:T(2,128)(2,1)} %reshape.86), calls=%async_computation.2 | async-start | bytes 32768 | tf_op jit(solution)/shard_map/all_to_all | solution.py:61
  92.7 28.0 %all_gather.15 = bf16[1024,128]{1,0:T(8,128)(2,1)S(1)} all-gather(bf16[64,128]{1,0:T(8,128)(2,1)S(1)} %bitcast.118), channel_id=1, replica_groups=mesh['row'=16,'col'=8] {'row'}, dimensions={0}, use_global_device_ids=true | all-gather | bytes 278528 | tf_op jit(solution)/shard_map/all_gather | solution.py:87
  120.6 0.0 all-to-all-done.2
  120.6 0.1 reshape.87
  120.7 25.4 %all_gather.14 = bf16[1024,64]{1,0:T(8,128)(2,1)S(1)} all-gather(bf16[128,64]{1,0:T(8,128)(2,1)S(1)} %bitcast_bitcast_fusion), channel_id=1, replica_groups=mesh['row'=16,'col'=8] {'col'}, dimensions={0}, use_global_device_ids=true | all-gather | bytes 147456 | tf_op jit(solution)/shard_map/all_gather | solution.py:65
  146.2 0.1 copy.56
  146.2 0.1 copy.57
  146.4 0.2 fusion.41
  146.5 0.6 all-gather.3.cloned.1.call-done
  147.1 15.5 %copy.49 = bf16[1024,64,32]{1,2,0:T(8,128)(2,1)} copy(bf16[1024,64,32]{0,2,1:T(8,128)(2,1)} %all-gather.3.cloned.1.call-done) | data formatting | bytes 8388608 | tf_op jit(solution)/shard_map/all_gather | solution.py:64
  162.7 15.8 %copy.50 = bf16[16,8,8,64,32]{4,3,2,1,0:T(8,128)(2,1)} copy(bf16[16,8,8,64,32]{3,4,2,0,1:T(8,128)(2,1)} %bitcast.104) | data formatting | bytes 8388608 | tf_op jit(solution)/shard_map/transpose | solution.py:77
  178.5 17.7 %copy.58 = bf16[4,1024,16,32]{1,3,2,0:T(8,128)(2,1)} copy(bf16[4,1024,16,32]{3,2,0,1:T(8,128)(2,1)} %bitcast.103) | data formatting | bytes 8388608 | tf_op jit(solution)/shard_map/while | solution.py:104
  196.2 28.1 %all-gather.5.cloned.1.call-done = bf16[1024,128,32]{1,2,0:T(8,128)(2,1)} async-done(((bf16[64,128,32]{1,2,0:T(8,128)(2,1)}), bf16[1024,128,32]{1,2,0:T(8,128)(2,1)}) %all-gather.5.cloned.1.call-update) | async-done | bytes 8388624 | tf_op jit(solution)/shard_map/all_gather | solution.py:86
  224.3 13.6 %copy.54 = bf16[1024,128,32]{0,2,1:T(8,128)(2,1)} copy(bf16[1024,128,32]{1,2,0:T(8,128)(2,1)} %all-gather.5.cloned.1.call-done) | data formatting | bytes 16777216 | tf_op jit(solution)/shard_map/all_gather | solution.py:86
  238.0 0.0 copy-done.10
  238.0 73.3 %while.10 = (s32[]{:T(128)}, bf16[4,16,128,128]{3,2,1,0:T(8,128)(2,1)}, bf16[4,1024,16,32]{1,3,2,0:T(8,128)(2,1)}, bf16[1024,4096]{0,1:T(8,128)(2,1)}, f32[4,16,...) while((s32[]{:T(128)}, bf16[4,16,128,128]{3,2,1,0:T(8,128)(2,1)}, ...), condition=%wide.region_3.4_spmd, body=%wide.region_2.3_spmd.sunk | while | flops 4836558848 | bytes 27027032 | solution.py:104
  238.0 16.2 %fusion.55 = f32[16,32,128,32]{2,1,3,0:T(8,128)S(1)} fusion(bf16[128,32,1024]{2,1,0:T(8,128)(2,1)} %bitcast.110, bf16[4,1024,16,32]{1,3,2,0:T(8,128)(2,1)} %get-tuple-element.148, s32[]{:T(128)} %get-tuple-element.138), kind=kOutput, calls=%fused_computation.clone.1 | convolution fusion | flops 4294967296 | bytes 17826304 | tf_op jit(solution)/shard_map/while/body/eval_jaxpr/dot_general | solution.py:96
  254.2 2.1 fusion.56
  256.3 16.2 %fusion.55 = f32[16,32,128,32]{2,1,3,0:T(8,128)S(1)} fusion(bf16[128,32,1024]{2,1,0:T(8,128)(2,1)} %bitcast.110, bf16[4,1024,16,32]{1,3,2,0:T(8,128)(2,1)} %get-tuple-element.148, s32[]{:T(128)} %get-tuple-element.138), kind=kOutput, calls=%fused_computation.clone.1 | convolution fusion | flops 4294967296 | bytes 17826304 | tf_op jit(solution)/shard_map/while/body/eval_jaxpr/dot_general | solution.py:96
  272.5 2.1 fusion.56
  274.6 16.2 %fusion.55 = f32[16,32,128,32]{2,1,3,0:T(8,128)S(1)} fusion(bf16[128,32,1024]{2,1,0:T(8,128)(2,1)} %bitcast.110, bf16[4,1024,16,32]{1,3,2,0:T(8,128)(2,1)} %get-tuple-element.148, s32[]{:T(128)} %get-tuple-element.138), kind=kOutput, calls=%fused_computation.clone.1 | convolution fusion | flops 4294967296 | bytes 17826304 | tf_op jit(solution)/shard_map/while/body/eval_jaxpr/dot_general | solution.py:96
  290.8 2.1 fusion.56
  293.0 16.2 %fusion.55 = f32[16,32,128,32]{2,1,3,0:T(8,128)S(1)} fusion(bf16[128,32,1024]{2,1,0:T(8,128)(2,1)} %bitcast.110, bf16[4,1024,16,32]{1,3,2,0:T(8,128)(2,1)} %get-tuple-element.148, s32[]{:T(128)} %get-tuple-element.138), kind=kOutput, calls=%fused_computation.clone.1 | convolution fusion | flops 4294967296 | bytes 17826304 | tf_op jit(solution)/shard_map/while/body/eval_jaxpr/dot_general | solution.py:96
  309.2 2.1 fusion.56
  311.3 0.7 copy-done.1
  (15 shorter events, 0.1 us)
Async XLA Ops:
  6.5 8.2 %copy-start = (bf16[256,32]{0,1:T(8,128)(2,1)S(1)}, bf16[256,32]{0,1:T(8,128)(2,1)}, u32[]{:S(2)}) copy-start(bf16[256,32]{0,1:T(8,128)(2,1)} %param.16) | copy-start | bytes 49156
  6.5 7.6 %copy-start.4 = (s32[8,1024]{1,0:T(8,128)S(1)}, s32[8,1024]{1,0:T(8,128)}, u32[]{:S(2)}) copy-start(s32[8,1024]{1,0:T(8,128)} %param.13) | copy-start | bytes 98308
  6.5 8.2 %copy-start.7 = (f32[256]{0:T(256)S(1)}, f32[256]{0:T(256)}, u32[]{:S(2)}) copy-start(f32[256]{0:T(256)} %param.14) | copy-start | bytes 3076
  6.5 8.2 %copy-start.6 = (f32[256]{0:T(256)S(1)}, f32[256]{0:T(256)}, u32[]{:S(2)}) copy-start(f32[256]{0:T(256)} %param.15) | copy-start | bytes 3076
  6.5 8.2 %copy-start.8 = (f32[32]{0:T(128)S(1)}, f32[32]{0:T(128)}, u32[]{:S(2)}) copy-start(f32[32]{0:T(128)} %param.17) | copy-start | bytes 388
  6.5 140.6 %all-gather.3.cloned.1.call-start = ((), (), s32[]{:S(2)}) async-start(), calls=%async_computation.4 | async-start | bytes 4718592 | tf_op jit(solution)/shard_map/all_gather | solution.py:64
  6.6 8.2 %copy-start.2 = (bf16[8,1024,256]{2,1,0:T(8,128)(2,1)S(1)}, bf16[8,1024,256]{2,1,0:T(8,128)(2,1)}, u32[]{:S(2)}) copy-start(bf16[8,1024,256]{2,1,0:T(8,128)(2,1)} %param.12) | copy-start | bytes 12582916
  18.6 27.8 %copy-start.5 = (bf16[256,32]{0,1:T(8,128)(2,1)S(1)}, bf16[256,32]{0,1:T(8,128)(2,1)}, u32[]{:S(2)}) copy-start(bf16[256,32]{0,1:T(8,128)(2,1)} %param.18) | copy-start | bytes 49156
  18.6 27.8 %copy-start.9 = (f32[32]{0:T(128)S(1)}, f32[32]{0:T(128)}, u32[]{:S(2)}) copy-start(f32[32]{0:T(128)} %param.19) | copy-start | bytes 388
  46.4 177.9 %all-gather.5.cloned.1.call-start = ((), (), s32[]{:S(2)}) async-start(), calls=%async_computation.5 | async-start | bytes 8912896 | tf_op jit(solution)/shard_map/all_gather | solution.py:86
  50.7 31.9 %copy-start.3 = (bf16[1024,128]{1,0:T(8,128)(2,1)S(1)}, bf16[1024,128]{1,0:T(8,128)(2,1)}, u32[]{:S(2)}) copy-start(bf16[1024,128]{1,0:T(8,128)(2,1)} %param.20) | copy-start | bytes 786436
  77.7 8.3 %all-to-all-start.3 = ((bf16[8,8,128]{2,0,1:T(8,128)(2,1)}), bf16[8,8,128]{2,0,1:T(8,128)(2,1)S(1)}, u32[]{:S(2)}, u32[]{:S(2)}) async-start(bf16[8,8,128]{2,0,1:T(8,128)(2,1)} %bitcast.34), calls=%async_computation.3 | async-start | bytes 32768 | tf_op jit(solution)/shard_map/all_to_all | solution.py:69
  86.1 34.5 %all-to-all-start.2 = ((bf16[16,2,256]{2,1,0:T(2,128)(2,1)}), bf16[16,2,256]{2,1,0:T(2,128)(2,1)S(1)}, u32[]{:S(2)}, u32[]{:S(2)}) async-start(bf16[16,2,256]{2,1,0:T(2,128)(2,1)} %reshape.86), calls=%async_computation.2 | async-start | bytes 32768 | tf_op jit(solution)/shard_map/all_to_all | solution.py:61
  196.2 41.8 %copy-start.10 = (f32[128]{0:T(128)S(1)}, f32[128]{0:T(128)}, u32[]{:S(2)}) copy-start(f32[128]{0:T(128)} %param.21) | copy-start | bytes 1540
  311.3 0.7 copy-start.1
Sparse Core Ops, SparseCore 0:
  46.5 100.5 all-gather.2
  149.6 74.6 all-gather.4
where the time goes:
time: 320 us; the launch traced here: 319 us
  blocking collectives  93.5 us (29%)
  matrix products  81.5 us (25%)
  local copies, waits for them, and re-layouts  80 us (25%)
  waiting for transfers between devices  32.2 us (10%)
  between operations  13.7 us (4%)
  starting transfers between devices  9.91 us (3%)
  other arithmetic  8.15 us (3%)
    dot_general x4, matrix products, one_block(): lax.dot_general(left_blk.reshape(seqs, block * width), right_flat, (((0,)...  64.7 us
    all_gather x1, waiting for transfers between devices, shards(): lax.all_gather(right_part, 'row', axis=0, tiled=True)  28.1 us
    all_gather x1, blocking collectives, shards(): lax.all_gather(right_mpart, 'row', axis=0, tiled=True)  28 us
    all_gather x1, blocking collectives, shards(): lax.all_gather(left_mpart, 'col', axis=0, tiled=True)  25.4 us
    all_to_all x1, blocking collectives, shards(): lax.all_to_all(transmit_second, 'col', split_axis=1, concat_axis=0, tiled...  20.6 us
    all_to_all x1, blocking collectives, shards(): lax.all_to_all(transmit_first, 'row', split_axis=1, concat_axis=0, tiled=...  19.5 us
    while x2, local copies, waits for them, and re-layouts, shards(): result = lax.map(one_block, (left_blocks, count_blocks))  17.8 us
    transpose x1, local copies, waits for them, and re-layouts, shards(): jnp.swapaxes(left_all, 0, 1).reshape((seqs,) + left_all.shape[3:])  15.8 us
  transfers between devices with their start and end apart: 4, of which 3 were waited for; matrix products, arithmetic and copies ran while one was open for 19% of the time, Pallas kernels for 0%

commit v1 on v0

v1 whole, which is shorter than its diff:
```python
import jax
import jax.numpy as jnp
from jax import lax
from jax.experimental import pallas as pl
from jax.experimental.pallas import tpu as pltpu
from jax.sharding import PartitionSpec as P

F32 = jnp.float32
BF16 = jnp.bfloat16
MESH = pl.DeviceIdType.MESH

SEQS = 8
RES = 1024
CH = 256
HALF = 16
GROUPS = 4
NI = 64 // GROUPS
NE = HALF // GROUPS
PIECE = (HALF + 2) * SEQS
DEPTH = 128


def column(row, n):
    eye = lax.broadcasted_iota(jnp.int32, (n, n), 0) == lax.broadcasted_iota(jnp.int32, (n, n), 1)
    return jnp.sum(jnp.where(eye, jnp.broadcast_to(row, (n, n)), 0.0), axis=1, keepdims=True)


def kernel(
    x_hbm, m_ref, gain_ref, off_ref, w1_ref, b1_ref, w2_ref, b2_ref, ft_ref, fo_ref,
    out_hbm,
    xv, wst, cst, stage, sbuf, abuf, t2, tm, lg, ls, rg, rs, lm, rm, mid, acc, cnt, ob,
    xsem, asend, arecv, gsend, grecv, ssend, srecv, msend, mrecv, osem,
):
    row = lax.axis_index("row")
    col = lax.axis_index("col")
    core = lax.rem(row, 2)
    sibling = row + 1 - 2 * core
    own = (col, row // 2)
    place = (row, col * 2 + core)

    def exchange_id(mat, p):
        return (p, col) if mat == 0 else ((row // 2) * 2 + lax.rem(p, 2), p // 2)

    def gather_id(mat, k):
        return (row, k) if mat == 0 else (k * 2 + core, col)

    barrier = pltpu.get_barrier_semaphore()

    def hello(d, c):
        pl.semaphore_signal(barrier, inc=1, device_id=exchange_id(0, lax.rem(row + d, 16)), device_id_type=MESH)
        return c

    def hello_cols(d, c):
        k = lax.rem(col + d, 8)
        pl.semaphore_signal(barrier, inc=1, device_id=(row, k), device_id_type=MESH)
        pl.semaphore_signal(barrier, inc=1, device_id=(sibling, k), device_id_type=MESH)
        return c

    lax.fori_loop(1, 16, hello, 0)
    lax.fori_loop(1, 8, hello_cols, 0)

    def xcopy(s):
        return pltpu.make_async_copy(x_hbm.at[s], xv.at[s], xsem.at[s])

    for s in range(SEQS):
        xcopy(s).start()

    wt = jnp.concatenate([w1_ref[...].astype(F32).T, w2_ref[...].astype(F32).T], axis=0)
    gw = wt * gain_ref[...]
    hi = gw.astype(BF16)
    lo = (gw - hi.astype(F32)).astype(BF16)
    wst[0:64] = hi
    wst[64:128] = lo
    wst[128:144] = jnp.ones((16, CH), BF16)
    cst[0] = jnp.broadcast_to(jnp.sum(hi.astype(F32) + lo.astype(F32), axis=1, keepdims=True), (64, 128))
    bias = jnp.concatenate([column(b1_ref[...], 32), column(b2_ref[...], 32)], axis=0)
    cst[1] = jnp.broadcast_to(jnp.sum(wt * off_ref[...], axis=1, keepdims=True) + bias, (64, 128))

    def project(s, c):
        xcopy(s).wait()
        x = xv[s]
        p = lax.dot_general(wst[...], x, (((1,), (1,)), ((), ())), preferred_element_type=F32)
        mean_rows = jnp.dot(x, jnp.ones((CH, 128), BF16), preferred_element_type=F32) * (1.0 / CH)
        xf = x.astype(F32)
        d0 = xf[:, :128] - mean_rows
        d1 = xf[:, 128:] - mean_rows
        sq = jnp.concatenate([(d0 * d0).astype(BF16), (d1 * d1).astype(BF16)], axis=1)
        v = lax.dot_general(jnp.ones((16, CH), BF16), sq, (((1,), (1,)), ((), ())), preferred_element_type=F32)
        for t in range(8):
            lanes = slice(t * 128, (t + 1) * 128)
            mean = p[128:129, lanes] * (1.0 / CH)
            scale = lax.rsqrt(v[0:1, lanes] * (1.0 / CH) + 1e-5)
            y = (p[0:64, lanes] + p[64:128, lanes] - mean * cst[0]) * scale + cst[1]
            stage[t, pl.ds(s, 64, stride=SEQS), :] = y
        return c

    lax.fori_loop(0, SEQS, project, 0)

    for t in range(8):
        mask = m_ref[:, t * 128 : (t + 1) * 128].astype(F32)
        mask2 = jnp.concatenate([mask, mask], axis=0).astype(BF16)
        for mat in range(2):
            for h in range(2):
                at = mat * 256 + h * 128
                y = stage[t, at : at + 128, :].reshape(HALF, SEQS, 128) * mask
                sbuf[mat, t * 2 + h, 0:128, :] = y.reshape(128, 128).astype(BF16)
                sbuf[mat, t * 2 + h, 128:144, :] = mask2

    pl.semaphore_wait(barrier, 29)

    def acopy(mat, p):
        return pltpu.make_async_remote_copy(
            src_ref=sbuf.at[mat, p], dst_ref=abuf.at[mat, place[mat]],
            send_sem=asend.at[mat, p], recv_sem=arecv.at[mat, place[mat]],
            device_id=exchange_id(mat, p), device_id_type=MESH)

    def aland(mat, p):
        return pltpu.make_async_remote_copy(
            src_ref=sbuf.at[mat, p], dst_ref=abuf.at[mat, p],
            send_sem=asend.at[mat, p], recv_sem=arecv.at[mat, p],
            device_id=exchange_id(mat, p), device_id_type=MESH)

    def asend_all(d, c):
        for mat in range(2):
            acopy(mat, lax.rem(place[mat] + d, 16)).start()
        return c

    lax.fori_loop(1, 16, asend_all, 0)
    for mat in range(2):
        abuf[mat, place[mat]] = sbuf[mat, place[mat]]
    acc[...] = jnp.zeros_like(acc)

    def await_all(mat):
        def one(d, c):
            aland(mat, lax.rem(place[mat] + d, 16)).wait_recv()
            return c

        lax.fori_loop(1, 16, one, 0)

    def slot(mat, g, k):
        return lg.at[g, k] if mat == 0 else rg.at[g, :, k]

    def gcopy(mat, g, k, to, n):
        return pltpu.make_async_remote_copy(
            src_ref=slot(mat, g, k), dst_ref=slot(mat, g, k),
            send_sem=gsend.at[mat, g, n], recv_sem=grecv.at[mat, g, k],
            device_id=gather_id(mat, to), device_id_type=MESH)

    def scopy(mat, g, k):
        src = lg.at[g, k, 1] if mat == 0 else rg.at[g, :, k]
        dst = ls.at[g, k] if mat == 0 else rs.at[g, :, k]
        return pltpu.make_async_remote_copy(
            src_ref=src, dst_ref=dst,
            send_sem=ssend.at[mat, g, k], recv_sem=srecv.at[mat, g, k],
            device_id=(sibling, col), device_id_type=MESH)

    def mslot(mat, k):
        return lm.at[k] if mat == 0 else rm.at[:, k]

    def mcopy(mat, k, to):
        return pltpu.make_async_remote_copy(
            src_ref=mslot(mat, k), dst_ref=mslot(mat, k),
            send_sem=msend.at[mat, to], recv_sem=mrecv.at[mat, k],
            device_id=gather_id(mat, to), device_id_type=MESH)

    mate = tuple(k + 1 - 2 * lax.rem(k, 2) for k in own)

    def ring(k, steps):
        return lax.rem(k + 2 * steps, 8)

    def to_mate(mat, g):
        gcopy(mat, g, own[mat], mate[mat], 0).start()

    def to_ring(mat, g):
        k = own[mat]
        gcopy(mat, g, k, ring(k, 1), 1).start()
        gcopy(mat, g, k, ring(k, 3), 2).start()
        scopy(mat, g, k).start()

    def landed(mat, g, k):
        gcopy(mat, g, k, mate[mat], 0).wait_recv()

    def s1(mat, g):
        k = own[mat]
        landed(mat, g, mate[mat])
        gcopy(mat, g, mate[mat], ring(k, 1), 3).start()
        gcopy(mat, g, mate[mat], ring(k, 3), 4).start()
        scopy(mat, g, mate[mat]).start()

    def s2(mat, g):
        k = own[mat]
        landed(mat, g, ring(k, 3))
        gcopy(mat, g, ring(k, 3), ring(k, 1), 5).start()
        landed(mat, g, ring(k, 1))
        scopy(mat, g, ring(k, 3)).start()
        scopy(mat, g, ring(k, 1)).start()

    def s3(mat, g):
        k = own[mat]
        landed(mat, g, ring(mate[mat], 1))
        gcopy(mat, g, ring(mate[mat], 1), ring(k, 3), 6).start()
        landed(mat, g, ring(mate[mat], 3))
        scopy(mat, g, ring(mate[mat], 1)).start()
        scopy(mat, g, ring(mate[mat], 3)).start()

    def s4(mat, g):
        for k in (ring(own[mat], 2), ring(mate[mat], 2)):
            landed(mat, g, k)
            scopy(mat, g, k).start()

    def s5(mat, g):
        def one(k, c):
            scopy(mat, g, k).wait_recv()
            return c

        lax.fori_loop(0, 8, one, 0)

    await_all(1)
    for pair in range(HALF // 2 + 1):
        part = abuf[1, :, pair * 16 : pair * 16 + 16, :].astype(F32).reshape(16, 2, 8, 128)
        for q in range(2):
            e = pair * 2 + q
            tile = part[:, q].reshape(8, 16, 128).astype(BF16)
            if e < HALF:
                at = (e % NE) * 128
                rg[e // NE, :, own[1], :, at : at + 128] = tile
            elif e == HALF:
                rm[:, own[1]] = tile
    for g in range(2):
        to_mate(1, g)
        to_ring(1, g)

    await_all(0)
    for pair in range(HALF // 2 + 1):
        part = abuf[0, :, pair * 16 : pair * 16 + 16, :].astype(F32).reshape(16, 2, 8, 128)
        for q in range(2):
            c = pair * 2 + q
            if c <= HALF:
                tile = part[:, q].reshape(128, 128).T
                if c < HALF:
                    t2[pl.ds(c, 128, stride=HALF), :] = tile
                else:
                    tm[...] = tile
    for g in range(GROUPS):
        for rel in range(2):
            half = core if rel == 0 else 1 - core
            rows = pl.multiple_of((half * 64 + g * NI) * HALF, NI * HALF)
            lg[g, own[0], rel] = t2[pl.ds(rows, NI * HALF), :].astype(BF16)
    lm[own[0]] = tm[pl.ds(pl.multiple_of(core * 64, 64), 64), :].astype(BF16)
    for g in range(2):
        to_mate(0, g)
        to_ring(0, g)
    for mat in range(2):
        for g in range(2, GROUPS):
            to_mate(mat, g)

    def send_masks(d, c):
        for mat in range(2):
            mcopy(mat, own[mat], lax.rem(own[mat] + d, 8)).start()
        return c

    lax.fori_loop(1, 8, send_masks, 0)

    def block(gl, gr):
        for rh in range(2):
            rhs = (rg if rh == 0 else rs)[gr].reshape(1024, NE * 128)
            for lh in range(2):
                lhs = jnp.concatenate([lg[gl, k, 0] if lh == 0 else ls[gl, k] for k in range(8)], axis=1)
                o = jnp.dot(lhs, rhs, preferred_element_type=F32).astype(BF16)
                for e in range(NE):
                    at = ((rh * NE + e) * 2 + lh) * 16
                    for i in range(NI):
                        mid[at : at + 16, i * 128 : (i + 1) * 128] = o[i * 16 : (i + 1) * 16, e * 128 : (e + 1) * 128]
        acc[gl] += jnp.dot(ft_ref[gr], mid[...], preferred_element_type=F32)

    def ocopy(gl):
        return pltpu.make_async_copy(ob.at[gl], out_hbm.at[pl.ds(gl * NI, NI)], osem.at[gl])

    def finish(gl):
        offset = jnp.broadcast_to(column(fo_ref[...], DEPTH), (DEPTH, 128))

        def one(i, c):
            lanes = pl.ds(pl.multiple_of(i * 128, 128), 128)
            y = acc[gl, :, lanes] * cnt[pl.ds(gl * NI + i, 1), :] + offset
            ob[gl, i] = y.T.astype(BF16)
            return c

        lax.fori_loop(0, NI, one, 0)
        ocopy(gl).start()

    both = (0, 1)

    def serve(f, g):
        for mat in both:
            f(mat, g)

    def compute(g, last=False):
        def along_right(r, c):
            block(g, r)
            return c

        def along_left(l, c):
            block(l, g)
            if last:
                finish(l)
            return c

        lax.fori_loop(0, g + 1, along_right, 0)
        if last:
            finish(g)
        if g > 0:
            lax.fori_loop(0, g, along_left, 0)

    for f in (s1, s2, s3):
        serve(f, 0)
    serve(to_ring, 2)
    for f in (s1, s2, s3):
        serve(f, 1)
    serve(s4, 0)
    serve(s5, 0)
    compute(0)
    serve(to_ring, 3)
    for f in (s1, s2, s3):
        serve(f, 2)
    serve(s4, 1)
    serve(s5, 1)
    compute(1)
    for f in (s1, s2, s3):
        serve(f, 3)
    serve(s4, 2)
    serve(s5, 2)

    def await_masks(d, c):
        for mat in both:
            k = lax.rem(own[mat] + d, 8)
            mcopy(mat, k, k).wait_recv()
        return c

    lax.fori_loop(1, 8, await_masks, 0)
    count = jnp.dot(
        jnp.concatenate([lm[k] for k in range(8)], axis=1), rm[...].reshape(1024, 128), preferred_element_type=F32)
    cnt[...] = 1.0 / (count + 0.001)

    compute(2)
    serve(s4, 3)
    serve(s5, 3)
    compute(3, last=True)

    def asent(d, c):
        for mat in both:
            acopy(mat, lax.rem(place[mat] + d, 16)).wait_send()
        return c

    def msent(d, c):
        for mat in both:
            mcopy(mat, own[mat], lax.rem(own[mat] + d, 8)).wait_send()
        return c

    def gsent(g, c):
        for mat in both:
            for n in range(7):
                gcopy(mat, g, own[mat], mate[mat], n).wait_send()
            for k in range(8):
                scopy(mat, g, k).wait_send()
        return c

    lax.fori_loop(1, 16, asent, 0)
    lax.fori_loop(1, 8, msent, 0)
    lax.fori_loop(0, GROUPS, gsent, 0)
    for gl in range(GROUPS):
        ocopy(gl).wait()


def shards(x, mask, gain, off, w1, b1, w2, b2, final, final_offset):
    core = lax.rem(lax.axis_index("row"), 2)
    ft = final.reshape(2, HALF, 2, GROUPS, NE, DEPTH).transpose(3, 5, 2, 4, 0, 1)
    ft = jnp.where(core == 0, ft, ft[:, :, ::-1, :, ::-1, :]).reshape(GROUPS, DEPTH, 64 * NE)
    vmem = pl.BlockSpec(memory_space=pltpu.VMEM)
    hbm = pl.BlockSpec(memory_space=pl.ANY)
    dma = pltpu.SemaphoreType.DMA
    return pl.pallas_call(
        kernel,
        out_shape=jax.ShapeDtypeStruct((64, 128, DEPTH), BF16),
        in_specs=[hbm] + [vmem] * 9,
        out_specs=hbm,
        scratch_shapes=[
            pltpu.VMEM((SEQS, RES, CH), BF16),
            pltpu.VMEM((144, CH), BF16),
            pltpu.VMEM((2, 64, 128), F32),
            pltpu.VMEM((8, 64 * SEQS, 128), F32),
            pltpu.VMEM((2, 16, PIECE, 128), BF16),
            pltpu.VMEM((2, 16, PIECE, 128), BF16),
            pltpu.VMEM((128 * HALF, 128), F32),
            pltpu.VMEM((128, 128), F32),
            pltpu.VMEM((GROUPS, 8, 2, NI * HALF, 128), BF16),
            pltpu.VMEM((GROUPS, 8, NI * HALF, 128), BF16),
            pltpu.VMEM((GROUPS, 8, 8, 16, NE * 128), BF16),
            pltpu.VMEM((GROUPS, 8, 8, 16, NE * 128), BF16),
            pltpu.VMEM((8, 64, 128), BF16),
            pltpu.VMEM((8, 8, 16, 128), BF16),
            pltpu.VMEM((64 * NE, NI * 128), BF16),
            pltpu.VMEM((GROUPS, DEPTH, NI * 128), F32),
            pltpu.VMEM((64, 128), F32),
            pltpu.VMEM((GROUPS, NI, 128, DEPTH), BF16),
            dma((SEQS,)),
            dma((2, 16)),
            dma((2, 16)),
            dma((2, GROUPS, 8)),
            dma((2, GROUPS, 8)),
            dma((2, GROUPS, 8)),
            dma((2, GROUPS, 8)),
            dma((2, 8)),
            dma((2, 8)),
            dma((GROUPS,)),
        ],
        compiler_params=pltpu.CompilerParams(
            collective_id=0, has_side_effects=True, vmem_limit_bytes=56 * 1024 * 1024),
        cost_estimate=pl.CostEstimate(flops=20_000_000_000, bytes_accessed=8_000_000, transcendentals=0),
    )(x, mask, gain.reshape(1, CH), off.reshape(1, CH), w1, b1.reshape(1, 32), w2, b2.reshape(1, 32), ft,
      final_offset.reshape(1, DEPTH))


def solution(mesh):
    every = P(("row", "col"))
    in_specs = (every, every) + (P(),) * 8
    return jax.shard_map(shards, mesh=mesh, in_specs=in_specs, out_specs=P("row", "col", None), check_vma=False)
```

time: 320 us -> 117 us (0.37)
  Pallas kernels: 0 us -> 108 us
  blocking collectives: 93.5 us -> 0 us
  matrix products: 81.5 us -> 0 us
  local copies, waits for them, and re-layouts: 80 us -> 6.99 us
  waiting for transfers between devices: 32.2 us -> 0 us
  between operations: 13.7 us -> 0.02 us
  starting transfers between devices: 9.91 us -> 0 us
  other arithmetic: 8.15 us -> 1.23 us
    pallas_call x0 -> x1, Pallas kernels: none -> 108 us  [shards(): pl.pallas_call(kernel, out_shape=jax.ShapeDtypeStruct((64, 128, DEPTH), B...]
    dot_general x11 -> x0, matrix products: 81.5 us -> none  [the longest x4 64.7 us: one_block(): lax.dot_general(left_blk.reshape(seqs, block * width), right_flat, (((0,)...]
    all_gather x2 -> x0, blocking collectives: 53.4 us -> none  [the longest x1 28 us: shards(): lax.all_gather(right_mpart, 'row', axis=0, tiled=True)]
    all_to_all x2 -> x0, blocking collectives: 40.1 us -> none  [the longest x1 20.6 us: shards(): lax.all_to_all(transmit_second, 'col', split_axis=1, concat_axis=0, tiled...]
    all_gather x2 -> x0, local copies, waits for them, and re-layouts: 29.2 us -> none  [the longest x1 15.5 us: shards(): lax.all_gather(left_part, 'col', axis=0, tiled=True)]
    all_gather x2 -> x0, waiting for transfers between devices: 28.7 us -> none  [the longest x1 28.1 us: shards(): lax.all_gather(right_part, 'row', axis=0, tiled=True)]
    while x2 -> x0, local copies, waits for them, and re-layouts: 17.8 us -> none  [shards(): result = lax.map(one_block, (left_blocks, count_blocks))]
    transpose x2 -> x0, local copies, waits for them, and re-layouts: 15.9 us -> none  [the longest x1 15.8 us: shards(): jnp.swapaxes(left_all, 0, 1).reshape((seqs,) + left_all.shape[3:])]
  transfers between devices with their start and end apart: 4 -> 0, of which waited for: 3 -> 0; matrix products, arithmetic and copies ran while one was open for 19% -> 0% of each run, Pallas kernels for 0% -> 0%
where the time goes in v1:
time: 117 us; the launch traced here: 116 us
  Pallas kernels  108 us (92%)
  local copies, waits for them, and re-layouts  6.99 us (6%)
  other arithmetic  1.23 us (1%)
    pallas_call x1, Pallas kernels, shards(): pl.pallas_call(kernel, out_shape=jax.ShapeDtypeStruct((64, 128, DEPTH), B...  108 us
    unnamed x3, local copies, waits for them, and re-layouts  6.03 us

profile of v1, /device:TPU:1, one launch (start us, length us, event | category | flops | bytes accessed | tf_op | source)
XLA Modules:
  0.0 116.1 jit_solution(7770729784721627426)
XLA Ops:
  0.0 1.4 %copy.18.w1_ref = bf16[256,32]{1,0:T(8,128)(2,1)} copy(bf16[256,32]{0,1:T(8,128)(2,1)} %param.14) | data formatting | bytes 32768 | tf_op args[4]
  1.4 1.4 %copy.19.w2_ref = bf16[256,32]{1,0:T(8,128)(2,1)} copy(bf16[256,32]{0,1:T(8,128)(2,1)} %param.16) | data formatting | bytes 32768 | tf_op args[6]
  2.9 1.2 %reverse_select_fusion = bf16[4,128,2,4,2,16]{1,3,0,2,5,4:T(4,128)(2,1)S(1)} fusion(bf16[4,128,2,4,2,16]{1,3,0,2,5,4:T(4,128)(2,1)} %bitcast.10, pred[]{:T(512)S(6)} %eq.3), kind=kLoop, calls=%fused_computation | loop fusion | flops 131072 | bytes 524289 | tf_op jit(solution)/shard_map/jit(_where)/select_n | solution.py:377
  4.1 0.1 copy.17
  4.2 0.9 copy.20.ft_ref
  5.1 107.8 %shard_map.100 = bf16[64,128,128]{2,1,0:T(8,128)(2,1)} custom-call(bf16[8,1024,256]{2,1,0:T(8,128)(2,1)} %x_hbm.1, s32[8,1024]{1,0:T(8,128)} %m_ref.1, f32[1,256]{1,0:T(1,128)} %bitcast.11, f32[1,256]{1,0:T(1,128)} %bitcast.12, bf16[256,32]{1,0:T(8,128)(2,1)} %copy.18.w1_ref, f32[1,32]{1,0:T(1,128)} %bitcast.13, bf16[256,32]{1,0:T(8,128)(2,1)} %copy.19.w2_ref, ...), custom_call_target="tpu_custom_call" | custom-call | flops 20000000000 | bytes 8000000 | tf_op jit(solution)/shard_map/pallas_call | solution.py:381
  112.9 3.2 %copy.22 = bf16[64,128,128]{2,1,0:T(8,128)(2,1)} copy(bf16[64,128,128]{2,1,0:T(8,128)(2,1)} %shard_map.100) | data formatting | bytes 4194304

commit v2 on v1

--- a/solution.py
+++ b/solution.py
@@ -26,9 +26,9 @@
 
 
 def kernel(
-    x_hbm, m_ref, gain_ref, off_ref, w1_ref, b1_ref, w2_ref, b2_ref, ft_ref, fo_ref,
+    x_hbm, m_ref, gain_ref, off_ref, w1_ref, b1_ref, w2_ref, b2_ref, f_ref, fo_ref,
     out_hbm,
-    xv, wst, cst, stage, sbuf, abuf, t2, tm, lg, ls, rg, rs, lm, rm, mid, acc, cnt, ob,
+    xv, wst, cst, fsc, ft_ref, stage, sbuf, abuf, t2, tm, lg, ls, rg, rs, lm, rm, mid, acc, cnt, ob,
     xsem, asend, arecv, gsend, grecv, ssend, srecv, msend, mrecv, osem,
 ):
     row = lax.axis_index("row")
@@ -65,7 +65,7 @@
     for s in range(SEQS):
         xcopy(s).start()
 
-    wt = jnp.concatenate([w1_ref[...].astype(F32).T, w2_ref[...].astype(F32).T], axis=0)
+    wt = jnp.concatenate([w1_ref[...].astype(F32), w2_ref[...].astype(F32)], axis=0)
     gw = wt * gain_ref[...]
     hi = gw.astype(BF16)
     lo = (gw - hi.astype(F32)).astype(BF16)
@@ -130,6 +130,17 @@
         abuf[mat, place[mat]] = sbuf[mat, place[mat]]
     acc[...] = jnp.zeros_like(acc)
 
+    fsc[...] = f_ref[...].astype(F32)
+    for g in range(GROUPS):
+        parts = []
+        for rh in range(2):
+            for e in range(NE):
+                for lh in range(2):
+                    re = rh + core - 2 * rh * core
+                    le = lh + core - 2 * lh * core
+                    parts.append(fsc[pl.ds(le * 512 + re * HALF + (g * NE + e), HALF, stride=32), :])
+        ft_ref[g] = jnp.concatenate(parts, axis=0).T.astype(BF16)
+
     def await_all(mat):
         def one(d, c):
             aland(mat, lax.rem(place[mat] + d, 16)).wait_recv()
@@ -191,17 +202,16 @@
         k = own[mat]
         landed(mat, g, ring(k, 3))
         gcopy(mat, g, ring(k, 3), ring(k, 1), 5).start()
-        landed(mat, g, ring(k, 1))
         scopy(mat, g, ring(k, 3)).start()
-        scopy(mat, g, ring(k, 1)).start()
 
     def s3(mat, g):
         k = own[mat]
         landed(mat, g, ring(mate[mat], 1))
         gcopy(mat, g, ring(mate[mat], 1), ring(k, 3), 6).start()
-        landed(mat, g, ring(mate[mat], 3))
         scopy(mat, g, ring(mate[mat], 1)).start()
-        scopy(mat, g, ring(mate[mat], 3)).start()
+        for other in (ring(k, 1), ring(mate[mat], 3)):
+            landed(mat, g, other)
+            scopy(mat, g, other).start()
 
     def s4(mat, g):
         for k in (ring(own[mat], 2), ring(mate[mat], 2)):
@@ -278,86 +288,68 @@
 
     def finish(gl):
         offset = jnp.broadcast_to(column(fo_ref[...], DEPTH), (DEPTH, 128))
-
-        def one(i, c):
-            lanes = pl.ds(pl.multiple_of(i * 128, 128), 128)
-            y = acc[gl, :, lanes] * cnt[pl.ds(gl * NI + i, 1), :] + offset
+        for i in range(NI):
+            y = acc[gl, :, i * 128 : (i + 1) * 128] * cnt[pl.ds(gl * NI + i, 1), :] + offset
             ob[gl, i] = y.T.astype(BF16)
-            return c
-
-        lax.fori_loop(0, NI, one, 0)
         ocopy(gl).start()
 
-    both = (0, 1)
-
     def serve(f, g):
-        for mat in both:
-            f(mat, g)
-
-    def compute(g, last=False):
-        def along_right(r, c):
+        if 0 <= g < GROUPS:
+            for mat in range(2):
+                f(mat, g)
+
+    def compute_right(g):
+        def one(r, c):
             block(g, r)
             return c
 
-        def along_left(l, c):
+        if 0 <= g < GROUPS:
+            lax.fori_loop(0, g + 1, one, 0)
+
+    def compute_left(g):
+        def one(l, c):
+            if g == GROUPS - 1:
+                finish(lax.rem(l + GROUPS - 1, GROUPS))
             block(l, g)
-            if last:
-                finish(l)
             return c
 
-        lax.fori_loop(0, g + 1, along_right, 0)
-        if last:
-            finish(g)
-        if g > 0:
-            lax.fori_loop(0, g, along_left, 0)
-
-    for f in (s1, s2, s3):
-        serve(f, 0)
-    serve(to_ring, 2)
-    for f in (s1, s2, s3):
-        serve(f, 1)
-    serve(s4, 0)
-    serve(s5, 0)
-    compute(0)
-    serve(to_ring, 3)
-    for f in (s1, s2, s3):
-        serve(f, 2)
-    serve(s4, 1)
-    serve(s5, 1)
-    compute(1)
-    for f in (s1, s2, s3):
-        serve(f, 3)
-    serve(s4, 2)
-    serve(s5, 2)
+        if 0 < g < GROUPS:
+            lax.fori_loop(0, g, one, 0)
 
     def await_masks(d, c):
-        for mat in both:
+        for mat in range(2):
             k = lax.rem(own[mat] + d, 8)
             mcopy(mat, k, k).wait_recv()
         return c
 
-    lax.fori_loop(1, 8, await_masks, 0)
-    count = jnp.dot(
-        jnp.concatenate([lm[k] for k in range(8)], axis=1), rm[...].reshape(1024, 128), preferred_element_type=F32)
-    cnt[...] = 1.0 / (count + 0.001)
-
-    compute(2)
-    serve(s4, 3)
-    serve(s5, 3)
-    compute(3, last=True)
+    for r in range(GROUPS + 3):
+        serve(s5, r - 3)
+        compute_right(r - 3)
+        serve(s4, r - 2)
+        serve(s3, r - 1)
+        serve(s1, r)
+        serve(s2, r)
+        serve(to_ring, r + 2)
+        if r == GROUPS + 1:
+            lax.fori_loop(1, 8, await_masks, 0)
+            lmask = jnp.concatenate([lm[k] for k in range(8)], axis=1)
+            count = jnp.dot(lmask, rm[...].reshape(1024, 128), preferred_element_type=F32)
+            cnt[...] = 1.0 / (count + 0.001)
+        compute_left(r - 3)
+    finish(GROUPS - 2)
 
     def asent(d, c):
-        for mat in both:
+        for mat in range(2):
             acopy(mat, lax.rem(place[mat] + d, 16)).wait_send()
         return c
 
     def msent(d, c):
-        for mat in both:
+        for mat in range(2):
             mcopy(mat, own[mat], lax.rem(own[mat] + d, 8)).wait_send()
         return c
 
     def gsent(g, c):
-        for mat in both:
+        for mat in range(2):
             for n in range(7):
                 gcopy(mat, g, own[mat], mate[mat], n).wait_send()
             for k in range(8):
@@ -372,9 +364,6 @@
 
 
 def shards(x, mask, gain, off, w1, b1, w2, b2, final, final_offset):
-    core = lax.rem(lax.axis_index("row"), 2)
-    ft = final.reshape(2, HALF, 2, GROUPS, NE, DEPTH).transpose(3, 5, 2, 4, 0, 1)
-    ft = jnp.where(core == 0, ft, ft[:, :, ::-1, :, ::-1, :]).reshape(GROUPS, DEPTH, 64 * NE)
     vmem = pl.BlockSpec(memory_space=pltpu.VMEM)
     hbm = pl.BlockSpec(memory_space=pl.ANY)
     dma = pltpu.SemaphoreType.DMA
@@ -387,6 +376,8 @@
             pltpu.VMEM((SEQS, RES, CH), BF16),
             pltpu.VMEM((144, CH), BF16),
             pltpu.VMEM((2, 64, 128), F32),
+            pltpu.VMEM((1024, DEPTH), F32),
+            pltpu.VMEM((GROUPS, DEPTH, 64 * NE), BF16),
             pltpu.VMEM((8, 64 * SEQS, 128), F32),
             pltpu.VMEM((2, 16, PIECE, 128), BF16),
             pltpu.VMEM((2, 16, PIECE, 128), BF16),
@@ -416,8 +407,8 @@
         compiler_params=pltpu.CompilerParams(
             collective_id=0, has_side_effects=True, vmem_limit_bytes=56 * 1024 * 1024),
         cost_estimate=pl.CostEstimate(flops=20_000_000_000, bytes_accessed=8_000_000, transcendentals=0),
-    )(x, mask, gain.reshape(1, CH), off.reshape(1, CH), w1, b1.reshape(1, 32), w2, b2.reshape(1, 32), ft,
-      final_offset.reshape(1, DEPTH))
+    )(x, mask, gain.reshape(1, CH), off.reshape(1, CH), w1.T, b1.reshape(1, 32), w2.T, b2.reshape(1, 32),
+      final, final_offset.reshape(1, DEPTH))
 
 
 def solution(mesh):

time: 117 us -> 94.5 us (0.81)
  Pallas kernels: 108 us -> 89.7 us
  local copies, waits for them, and re-layouts: 6.99 us -> 3.16 us
  other arithmetic: 1.23 us -> 0 us
    pallas_call x1, Pallas kernels: 108 us -> 89.7 us  [shards(): pl.pallas_call(kernel, out_shape=jax.ShapeDtypeStruct((64, 128, DEPTH), B...]
    unnamed x3 -> x1, local copies, waits for them, and re-layouts: 6.03 us -> 3.16 us
    select_n x1 -> x0, other arithmetic: 1.23 us -> none  [shards(): jnp.where(core == 0, ft, ft[:, :, ::-1, :, ::-1, :])]
where the time goes in v2:
time: 94.5 us; the launch traced here: 92.9 us
  Pallas kernels  89.7 us (95%)
  local copies, waits for them, and re-layouts  3.16 us (3%)
    pallas_call x1, Pallas kernels, shards(): pl.pallas_call(kernel, out_shape=jax.ShapeDtypeStruct((64, 128, DEPTH), B...  89.7 us
    unnamed x1, local copies, waits for them, and re-layouts  3.16 us

profile of v2, /device:TPU:1, one launch (start us, length us, event | category | flops | bytes accessed | tf_op | source)
XLA Modules:
  0.0 92.9 jit_solution(3314277956007850439)
XLA Ops:
  0.0 89.7 %shard_map.100 = bf16[64,128,128]{2,1,0:T(8,128)(2,1)} custom-call(bf16[8,1024,256]{2,1,0:T(8,128)(2,1)} %x_hbm.1, s32[8,1024]{1,0:T(8,128)} %m_ref.1, f32[1,256]{1,0:T(1,128)} %bitcast.9, f32[1,256]{1,0:T(1,128)} %bitcast.10, bf16[32,256]{1,0:T(8,128)(2,1)} %bitcast.7, f32[1,32]{1,0:T(1,128)} %bitcast.11, bf16[32,256]{1,0:T(8,128)(2,1)} %bitcast.8, ...), custom_call_target="tpu_custom_call" | custom-call | flops 20000000000 | bytes 8000000 | tf_op jit(solution)/shard_map/pallas_call | solution.py:370
  89.8 3.2 %copy.12 = bf16[64,128,128]{2,1,0:T(8,128)(2,1)} copy(bf16[64,128,128]{2,1,0:T(8,128)(2,1)} %shard_map.100) | data formatting | bytes 4194304

commit v3 on v2

--- a/solution.py
+++ b/solution.py
@@ -14,9 +14,10 @@
 CH = 256
 HALF = 16
 GROUPS = 4
+GP = GROUPS // 2
+AHEAD = 4
 NI = 64 // GROUPS
 NE = HALF // GROUPS
-PIECE = (HALF + 2) * SEQS
 DEPTH = 128
 
 
@@ -28,7 +29,7 @@
 def kernel(
     x_hbm, m_ref, gain_ref, off_ref, w1_ref, b1_ref, w2_ref, b2_ref, f_ref, fo_ref,
     out_hbm,
-    xv, wst, cst, fsc, ft_ref, stage, sbuf, abuf, t2, tm, lg, ls, rg, rs, lm, rm, mid, acc, cnt, ob,
+    xv, wst, cst, fsc, ft_ref, stage, sbuf0, sbuf1, abuf0, abuf1, t2, tm, lg, rg, rs, lm, rm, mid, acc, cnt, ob,
     xsem, asend, arecv, gsend, grecv, ssend, srecv, msend, mrecv, osem,
 ):
     row = lax.axis_index("row")
@@ -96,57 +97,72 @@
 
     lax.fori_loop(0, SEQS, project, 0)
 
+    lane = lax.broadcasted_iota(jnp.int32, (64, 128), 1) // 32
     for t in range(8):
         mask = m_ref[:, t * 128 : (t + 1) * 128].astype(F32)
         mask2 = jnp.concatenate([mask, mask], axis=0).astype(BF16)
-        for mat in range(2):
-            for h in range(2):
-                at = mat * 256 + h * 128
-                y = stage[t, at : at + 128, :].reshape(HALF, SEQS, 128) * mask
-                sbuf[mat, t * 2 + h, 0:128, :] = y.reshape(128, 128).astype(BF16)
-                sbuf[mat, t * 2 + h, 128:144, :] = mask2
+        left = (stage[t, 0:256, :].reshape(32, SEQS, 128) * mask).reshape(8, 4, SEQS, 128)
+        turned = [
+            [x if k == 0 else pltpu.roll(x, 32 * k, 1) for k in range(4)]
+            for x in (left[:, b].reshape(64, 128) for b in range(4))
+        ]
+        for h in range(2):
+            right = (stage[t, 256 + h * 128 : 384 + h * 128, :].reshape(HALF, SEQS, 128) * mask).reshape(128, 128)
+            for part, buf in enumerate((sbuf0, sbuf1)):
+                q = h * 2 + part
+                y = turned[0][(0 - q) % 4]
+                for b in range(1, 4):
+                    y = jnp.where(lane == b, turned[b][(b - q) % 4], y)
+                buf[0, t * 2 + h, 0:64, :] = y.astype(BF16)
+                buf[1, t * 2 + h, 0:64, :] = right[part * 64 : part * 64 + 64].astype(BF16)
+            for mat in range(2):
+                sbuf1[mat, t * 2 + h, 64:80, :] = mask2
 
     pl.semaphore_wait(barrier, 29)
 
-    def acopy(mat, p):
+    sbuf, abuf = (sbuf0, sbuf1), (abuf0, abuf1)
+
+    def acopy(part, mat, p):
         return pltpu.make_async_remote_copy(
-            src_ref=sbuf.at[mat, p], dst_ref=abuf.at[mat, place[mat]],
-            send_sem=asend.at[mat, p], recv_sem=arecv.at[mat, place[mat]],
+            src_ref=sbuf[part].at[mat, p], dst_ref=abuf[part].at[mat, place[mat]],
+            send_sem=asend.at[part, mat, p], recv_sem=arecv.at[part, mat, place[mat]],
             device_id=exchange_id(mat, p), device_id_type=MESH)
 
-    def aland(mat, p):
+    def aland(part, mat, p):
         return pltpu.make_async_remote_copy(
-            src_ref=sbuf.at[mat, p], dst_ref=abuf.at[mat, p],
-            send_sem=asend.at[mat, p], recv_sem=arecv.at[mat, p],
+            src_ref=sbuf[part].at[mat, p], dst_ref=abuf[part].at[mat, p],
+            send_sem=asend.at[part, mat, p], recv_sem=arecv.at[part, mat, p],
             device_id=exchange_id(mat, p), device_id_type=MESH)
 
-    def asend_all(d, c):
-        for mat in range(2):
-            acopy(mat, lax.rem(place[mat] + d, 16)).start()
-        return c
-
-    lax.fori_loop(1, 16, asend_all, 0)
-    for mat in range(2):
-        abuf[mat, place[mat]] = sbuf[mat, place[mat]]
+    def exchange(part):
+        def one(d, c):
+            for mat in range(2):
+                acopy(part, mat, lax.rem(place[mat] + d, 16)).start()
+            return c
+
+        lax.fori_loop(1, 16, one, 0)
+        for mat in range(2):
+            abuf[part][mat, place[mat]] = sbuf[part][mat, place[mat]]
+
+    def exchanged(part, mat):
+        def one(d, c):
+            aland(part, mat, lax.rem(place[mat] + d, 16)).wait_recv()
+            return c
+
+        lax.fori_loop(1, 16, one, 0)
+
+    exchange(0)
+    exchange(1)
     acc[...] = jnp.zeros_like(acc)
 
     fsc[...] = f_ref[...].astype(F32)
     for g in range(GROUPS):
         parts = []
         for rh in range(2):
+            re = rh + core - 2 * rh * core
             for e in range(NE):
-                for lh in range(2):
-                    re = rh + core - 2 * rh * core
-                    le = lh + core - 2 * lh * core
-                    parts.append(fsc[pl.ds(le * 512 + re * HALF + (g * NE + e), HALF, stride=32), :])
+                parts.append(fsc[pl.ds(re * HALF + (g * NE + e), 32, stride=32), :])
         ft_ref[g] = jnp.concatenate(parts, axis=0).T.astype(BF16)
-
-    def await_all(mat):
-        def one(d, c):
-            aland(mat, lax.rem(place[mat] + d, 16)).wait_recv()
-            return c
-
-        lax.fori_loop(1, 16, one, 0)
 
     def slot(mat, g, k):
         return lg.at[g, k] if mat == 0 else rg.at[g, :, k]
@@ -157,13 +173,15 @@
             send_sem=gsend.at[mat, g, n], recv_sem=grecv.at[mat, g, k],
             device_id=gather_id(mat, to), device_id_type=MESH)
 
-    def scopy(mat, g, k):
-        src = lg.at[g, k, 1] if mat == 0 else rg.at[g, :, k]
-        dst = ls.at[g, k] if mat == 0 else rs.at[g, :, k]
+    def scopy(g, k):
         return pltpu.make_async_remote_copy(
-            src_ref=src, dst_ref=dst,
-            send_sem=ssend.at[mat, g, k], recv_sem=srecv.at[mat, g, k],
+            src_ref=rg.at[g, :, k], dst_ref=rs.at[g, :, k],
+            send_sem=ssend.at[g, k], recv_sem=srecv.at[g, k],
             device_id=(sibling, col), device_id_type=MESH)
+
+    def share(mat, g, k):
+        if mat == 1:
+            scopy(g, k).start()
 
     def mslot(mat, k):
         return lm.at[k] if mat == 0 else rm.at[:, k]
@@ -186,7 +204,7 @@
         k = own[mat]
         gcopy(mat, g, k, ring(k, 1), 1).start()
         gcopy(mat, g, k, ring(k, 3), 2).start()
-        scopy(mat, g, k).start()
+        share(mat, g, k)
 
     def landed(mat, g, k):
         gcopy(mat, g, k, mate[mat], 0).wait_recv()
@@ -194,93 +212,99 @@
     def s1(mat, g):
         k = own[mat]
         landed(mat, g, mate[mat])
+        if g + 2 < GROUPS:
+            to_mate(mat, g + 2)
         gcopy(mat, g, mate[mat], ring(k, 1), 3).start()
         gcopy(mat, g, mate[mat], ring(k, 3), 4).start()
-        scopy(mat, g, mate[mat]).start()
+        share(mat, g, mate[mat])
 
     def s2(mat, g):
         k = own[mat]
         landed(mat, g, ring(k, 3))
         gcopy(mat, g, ring(k, 3), ring(k, 1), 5).start()
-        scopy(mat, g, ring(k, 3)).start()
+        share(mat, g, ring(k, 3))
 
     def s3(mat, g):
         k = own[mat]
         landed(mat, g, ring(mate[mat], 1))
         gcopy(mat, g, ring(mate[mat], 1), ring(k, 3), 6).start()
-        scopy(mat, g, ring(mate[mat], 1)).start()
+        share(mat, g, ring(mate[mat], 1))
         for other in (ring(k, 1), ring(mate[mat], 3)):
             landed(mat, g, other)
-            scopy(mat, g, other).start()
+            share(mat, g, other)
 
     def s4(mat, g):
         for k in (ring(own[mat], 2), ring(mate[mat], 2)):
             landed(mat, g, k)
-            scopy(mat, g, k).start()
+            share(mat, g, k)
 
     def s5(mat, g):
         def one(k, c):
-            scopy(mat, g, k).wait_recv()
+            scopy(g, k).wait_recv()
             return c
 
-        lax.fori_loop(0, 8, one, 0)
-
-    await_all(1)
-    for pair in range(HALF // 2 + 1):
-        part = abuf[1, :, pair * 16 : pair * 16 + 16, :].astype(F32).reshape(16, 2, 8, 128)
-        for q in range(2):
-            e = pair * 2 + q
-            tile = part[:, q].reshape(8, 16, 128).astype(BF16)
-            if e < HALF:
+        if mat == 1:
+            lax.fori_loop(0, 8, one, 0)
+
+    def rows_of(part, mat, at):
+        return abuf[part][mat, :, at : at + 16, :].astype(F32).reshape(16, 2, 8, 128)
+
+    def prepare_right(part):
+        exchanged(part, 1)
+        for pair in range(4):
+            both = rows_of(part, 1, pair * 16)
+            for q in range(2):
+                e = part * 8 + pair * 2 + q
                 at = (e % NE) * 128
-                rg[e // NE, :, own[1], :, at : at + 128] = tile
-            elif e == HALF:
-                rm[:, own[1]] = tile
-    for g in range(2):
-        to_mate(1, g)
-        to_ring(1, g)
-
-    await_all(0)
-    for pair in range(HALF // 2 + 1):
-        part = abuf[0, :, pair * 16 : pair * 16 + 16, :].astype(F32).reshape(16, 2, 8, 128)
-        for q in range(2):
-            c = pair * 2 + q
-            if c <= HALF:
-                tile = part[:, q].reshape(128, 128).T
-                if c < HALF:
-                    t2[pl.ds(c, 128, stride=HALF), :] = tile
-                else:
-                    tm[...] = tile
-    for g in range(GROUPS):
-        for rel in range(2):
-            half = core if rel == 0 else 1 - core
-            rows = pl.multiple_of((half * 64 + g * NI) * HALF, NI * HALF)
-            lg[g, own[0], rel] = t2[pl.ds(rows, NI * HALF), :].astype(BF16)
-    lm[own[0]] = tm[pl.ds(pl.multiple_of(core * 64, 64), 64), :].astype(BF16)
-    for g in range(2):
-        to_mate(0, g)
-        to_ring(0, g)
-    for mat in range(2):
-        for g in range(2, GROUPS):
-            to_mate(mat, g)
+                rg[e // NE, :, own[1], :, at : at + 128] = both[:, q].reshape(8, 16, 128).astype(BF16)
+        if part == 1:
+            rm[:, own[1]] = rows_of(part, 1, 64)[:, 0].reshape(8, 16, 128).astype(BF16)
+
+    def prepare_left(part):
+        exchanged(part, 0)
+        for pair in range(4):
+            both = rows_of(part, 0, pair * 16)
+            for q in range(2):
+                tile = both[:, q].reshape(128, 128).T
+                for b in range(4):
+                    t2[pl.ds((pair * 2 + q) * 4 + b, 32, stride=32), :] = tile[b * 32 : b * 32 + 32]
+        for g in range(GP):
+            lg[part * GP + g, own[0]] = t2[g * NI * 32 : (g + 1) * NI * 32, :].astype(BF16)
+        if part == 1:
+            tm[...] = rows_of(part, 0, 64)[:, 0].reshape(128, 128).T
+            lm[own[0]] = tm[pl.ds(pl.multiple_of(core * 64, 64), 64), :].astype(BF16)
+
+    def begin(mat, part):
+        for g in range(part * GP, part * GP + GP):
+            if g < 2:
+                to_mate(mat, g)
+            if g < AHEAD:
+                to_ring(mat, g)
 
     def send_masks(d, c):
         for mat in range(2):
             mcopy(mat, own[mat], lax.rem(own[mat] + d, 8)).start()
         return c
 
+    prepare_right(0)
+    begin(1, 0)
+    prepare_left(0)
+    begin(0, 0)
+    prepare_right(1)
+    begin(1, 1)
+    prepare_left(1)
+    begin(0, 1)
     lax.fori_loop(1, 8, send_masks, 0)
 
     def block(gl, gr):
+        lhs = jnp.concatenate([lg[gl, k] for k in range(8)], axis=1)
         for rh in range(2):
             rhs = (rg if rh == 0 else rs)[gr].reshape(1024, NE * 128)
-            for lh in range(2):
-                lhs = jnp.concatenate([lg[gl, k, 0] if lh == 0 else ls[gl, k] for k in range(8)], axis=1)
-                o = jnp.dot(lhs, rhs, preferred_element_type=F32).astype(BF16)
-                for e in range(NE):
-                    at = ((rh * NE + e) * 2 + lh) * 16
-                    for i in range(NI):
-                        mid[at : at + 16, i * 128 : (i + 1) * 128] = o[i * 16 : (i + 1) * 16, e * 128 : (e + 1) * 128]
+            o = jnp.dot(lhs, rhs, preferred_element_type=F32).astype(BF16)
+            for e in range(NE):
+                at = (rh * NE + e) * 32
+                for i in range(NI):
+                    mid[at : at + 32, i * 128 : (i + 1) * 128] = o[i * 32 : (i + 1) * 32, e * 128 : (e + 1) * 128]
         acc[gl] += jnp.dot(ft_ref[gr], mid[...], preferred_element_type=F32)
 
     def ocopy(gl):
@@ -308,8 +332,6 @@
 
     def compute_left(g):
         def one(l, c):
-            if g == GROUPS - 1:
-                finish(lax.rem(l + GROUPS - 1, GROUPS))
             block(l, g)
             return c
 
@@ -322,25 +344,46 @@
             mcopy(mat, k, k).wait_recv()
         return c
 
-    for r in range(GROUPS + 3):
-        serve(s5, r - 3)
-        compute_right(r - 3)
-        serve(s4, r - 2)
-        serve(s3, r - 1)
-        serve(s1, r)
-        serve(s2, r)
-        serve(to_ring, r + 2)
-        if r == GROUPS + 1:
-            lax.fori_loop(1, 8, await_masks, 0)
-            lmask = jnp.concatenate([lm[k] for k in range(8)], axis=1)
-            count = jnp.dot(lmask, rm[...].reshape(1024, 128), preferred_element_type=F32)
-            cnt[...] = 1.0 / (count + 0.001)
-        compute_left(r - 3)
+    serve(s1, 0)
+    serve(s2, 0)
+    serve(s1, 1)
+    serve(s3, 0)
+    serve(s2, 1)
+    serve(s4, 0)
+    serve(s1, 2)
+    serve(s2, 2)
+    serve(s3, 1)
+    serve(s5, 0)
+    compute_right(0)
+    serve(s4, 1)
+    serve(s1, 3)
+    serve(s2, 3)
+    serve(s3, 2)
+    serve(s5, 1)
+    compute_right(1)
+    compute_left(1)
+    serve(s4, 2)
+    lax.fori_loop(1, 8, await_masks, 0)
+    lmask = jnp.concatenate([lm[k] for k in range(8)], axis=1)
+    count = jnp.dot(lmask, rm[...].reshape(1024, 128), preferred_element_type=F32)
+    cnt[...] = 1.0 / (count + 0.001)
+    serve(s3, 3)
+    serve(s5, 2)
+    compute_right(2)
+    serve(s4, 3)
+    compute_left(2)
+    serve(s5, 3)
+    for r in range(4):
+        block(3, r)
+    for l in range(3):
+        finish((l + 3) % 4)
+        block(l, 3)
     finish(GROUPS - 2)
 
     def asent(d, c):
         for mat in range(2):
-            acopy(mat, lax.rem(place[mat] + d, 16)).wait_send()
+            for part in range(2):
+                acopy(part, mat, lax.rem(place[mat] + d, 16)).wait_send()
         return c
 
     def msent(d, c):
@@ -352,8 +395,8 @@
         for mat in range(2):
             for n in range(7):
                 gcopy(mat, g, own[mat], mate[mat], n).wait_send()
-            for k in range(8):
-                scopy(mat, g, k).wait_send()
+        for k in range(8):
+            scopy(g, k).wait_send()
         return c
 
     lax.fori_loop(1, 16, asent, 0)
@@ -379,12 +422,13 @@
             pltpu.VMEM((1024, DEPTH), F32),
             pltpu.VMEM((GROUPS, DEPTH, 64 * NE), BF16),
             pltpu.VMEM((8, 64 * SEQS, 128), F32),
-            pltpu.VMEM((2, 16, PIECE, 128), BF16),
-            pltpu.VMEM((2, 16, PIECE, 128), BF16),
-            pltpu.VMEM((128 * HALF, 128), F32),
+            pltpu.VMEM((2, 16, 64, 128), BF16),
+            pltpu.VMEM((2, 16, 80, 128), BF16),
+            pltpu.VMEM((2, 16, 64, 128), BF16),
+            pltpu.VMEM((2, 16, 80, 128), BF16),
+            pltpu.VMEM((32 * 32, 128), F32),
             pltpu.VMEM((128, 128), F32),
-            pltpu.VMEM((GROUPS, 8, 2, NI * HALF, 128), BF16),
-            pltpu.VMEM((GROUPS, 8, NI * HALF, 128), BF16),
+            pltpu.VMEM((GROUPS, 8, NI * 32, 128), BF16),
             pltpu.VMEM((GROUPS, 8, 8, 16, NE * 128), BF16),
             pltpu.VMEM((GROUPS, 8, 8, 16, NE * 128), BF16),
             pltpu.VMEM((8, 64, 128), BF16),
@@ -394,12 +438,12 @@
             pltpu.VMEM((64, 128), F32),
             pltpu.VMEM((GROUPS, NI, 128, DEPTH), BF16),
             dma((SEQS,)),
-            dma((2, 16)),
-            dma((2, 16)),
+            dma((2, 2, 16)),
+            dma((2, 2, 16)),
             dma((2, GROUPS, 8)),
             dma((2, GROUPS, 8)),
-            dma((2, GROUPS, 8)),
-            dma((2, GROUPS, 8)),
+            dma((GROUPS, 8)),
+            dma((GROUPS, 8)),
             dma((2, 8)),
             dma((2, 8)),
             dma((GROUPS,)),

time: 94.5 us -> 86.8 us (0.919); the launches traced: 92.9 us -> 86.6 us
  Pallas kernels: 89.7 us -> 83.4 us
    pallas_call x1, Pallas kernels: 89.7 us -> 83.4 us  [shards(): pl.pallas_call(kernel, out_shape=jax.ShapeDtypeStruct((64, 128, DEPTH), B...]
where the time goes in v3:
time: 86.8 us; the launch traced here: 86.6 us
  Pallas kernels  83.4 us (96%)
  local copies, waits for them, and re-layouts  3.16 us (4%)
    pallas_call x1, Pallas kernels, shards(): pl.pallas_call(kernel, out_shape=jax.ShapeDtypeStruct((64, 128, DEPTH), B...  83.4 us
    unnamed x1, local copies, waits for them, and re-layouts  3.16 us

profile of v3, /device:TPU:1, one launch (start us, length us, event | category | flops | bytes accessed | tf_op | source)
XLA Modules:
  0.0 86.6 jit_solution(11603925816214135279)
XLA Ops:
  0.0 83.4 %shard_map.100 = bf16[64,128,128]{2,1,0:T(8,128)(2,1)} custom-call(bf16[8,1024,256]{2,1,0:T(8,128)(2,1)} %x_hbm.1, s32[8,1024]{1,0:T(8,128)} %m_ref.1, f32[1,256]{1,0:T(1,128)} %bitcast.9, f32[1,256]{1,0:T(1,128)} %bitcast.10, bf16[32,256]{1,0:T(8,128)(2,1)} %bitcast.7, f32[1,32]{1,0:T(1,128)} %bitcast.11, bf16[32,256]{1,0:T(8,128)(2,1)} %bitcast.8, ...), custom_call_target="tpu_custom_call" | custom-call | flops 20000000000 | bytes 8000000 | tf_op jit(solution)/shard_map/pallas_call | solution.py:413
  83.5 3.2 %copy.12 = bf16[64,128,128]{2,1,0:T(8,128)(2,1)} copy(bf16[64,128,128]{2,1,0:T(8,128)(2,1)} %shard_map.100) | data formatting | bytes 4194304

commit v4 on v3

--- a/solution.py
+++ b/solution.py
@@ -369,9 +369,11 @@
     cnt[...] = 1.0 / (count + 0.001)
     serve(s3, 3)
     serve(s5, 2)
-    compute_right(2)
+    for r in range(3):
+        block(2, r)
     serve(s4, 3)
-    compute_left(2)
+    for l in range(2):
+        block(l, 2)
     serve(s5, 3)
     for r in range(4):
         block(3, r)

time: 86.8 us -> 86 us (level)
  no operation moved by 1% of the time
where the time goes in v4:
time: 86 us; the launch traced here: 85.9 us
  Pallas kernels  82.7 us (96%)
  local copies, waits for them, and re-layouts  3.16 us (4%)
    pallas_call x1, Pallas kernels, shards(): pl.pallas_call(kernel, out_shape=jax.ShapeDtypeStruct((64, 128, DEPTH), B...  82.7 us
    unnamed x1, local copies, waits for them, and re-layouts  3.16 us

profile of v4, /device:TPU:1, one launch (start us, length us, event | category | flops | bytes accessed | tf_op | source)
XLA Modules:
  0.0 85.9 jit_solution(15515474095776027067)
XLA Ops:
  0.0 82.7 %shard_map.100 = bf16[64,128,128]{2,1,0:T(8,128)(2,1)} custom-call(bf16[8,1024,256]{2,1,0:T(8,128)(2,1)} %x_hbm.1, s32[8,1024]{1,0:T(8,128)} %m_ref.1, f32[1,256]{1,0:T(1,128)} %bitcast.9, f32[1,256]{1,0:T(1,128)} %bitcast.10, bf16[32,256]{1,0:T(8,128)(2,1)} %bitcast.7, f32[1,32]{1,0:T(1,128)} %bitcast.11, bf16[32,256]{1,0:T(8,128)(2,1)} %bitcast.8, ...), custom_call_target="tpu_custom_call" | custom-call | flops 20000000000 | bytes 8000000 | tf_op jit(solution)/shard_map/pallas_call | solution.py:415
  82.7 3.2 %copy.12 = bf16[64,128,128]{2,1,0:T(8,128)(2,1)} copy(bf16[64,128,128]{2,1,0:T(8,128)(2,1)} %shard_map.100) | data formatting | bytes 4194304

commit v5 on v4

--- a/solution.py
+++ b/solution.py
@@ -368,15 +368,17 @@
     count = jnp.dot(lmask, rm[...].reshape(1024, 128), preferred_element_type=F32)
     cnt[...] = 1.0 / (count + 0.001)
     serve(s3, 3)
+    block(2, 0)
+    block(2, 1)
     serve(s5, 2)
-    for r in range(3):
-        block(2, r)
+    block(2, 2)
     serve(s4, 3)
     for l in range(2):
         block(l, 2)
+    for r in range(3):
+        block(3, r)
     serve(s5, 3)
-    for r in range(4):
-        block(3, r)
+    block(3, 3)
     for l in range(3):
         finish((l + 3) % 4)
         block(l, 3)

time: 86 us -> 84.8 us (0.986)
  Pallas kernels: 82.7 us -> 81.5 us
    pallas_call x1, Pallas kernels: 82.7 us -> 81.5 us  [shards(): pl.pallas_call(kernel, out_shape=jax.ShapeDtypeStruct((64, 128, DEPTH), B...]
where the time goes in v5:
time: 84.8 us; the launch traced here: 84.7 us
  Pallas kernels  81.5 us (96%)
  local copies, waits for them, and re-layouts  3.16 us (4%)
    pallas_call x1, Pallas kernels, shards(): pl.pallas_call(kernel, out_shape=jax.ShapeDtypeStruct((64, 128, DEPTH), B...  81.5 us
    unnamed x1, local copies, waits for them, and re-layouts  3.16 us

profile of v5, /device:TPU:1, one launch (start us, length us, event | category | flops | bytes accessed | tf_op | source)
XLA Modules:
  0.0 84.7 jit_solution(151654637914024452)
XLA Ops:
  0.0 81.5 %shard_map.100 = bf16[64,128,128]{2,1,0:T(8,128)(2,1)} custom-call(bf16[8,1024,256]{2,1,0:T(8,128)(2,1)} %x_hbm.1, s32[8,1024]{1,0:T(8,128)} %m_ref.1, f32[1,256]{1,0:T(1,128)} %bitcast.9, f32[1,256]{1,0:T(1,128)} %bitcast.10, bf16[32,256]{1,0:T(8,128)(2,1)} %bitcast.7, f32[1,32]{1,0:T(1,128)} %bitcast.11, bf16[32,256]{1,0:T(8,128)(2,1)} %bitcast.8, ...), custom_call_target="tpu_custom_call" | custom-call | flops 20000000000 | bytes 8000000 | tf_op jit(solution)/shard_map/pallas_call | solution.py:417
  81.5 3.2 %copy.12 = bf16[64,128,128]{2,1,0:T(8,128)(2,1)} copy(bf16[64,128,128]{2,1,0:T(8,128)(2,1)} %shard_map.100) | data formatting | bytes 4194304

commit v6 on v5

--- a/solution.py
+++ b/solution.py
@@ -359,9 +359,10 @@
     serve(s1, 3)
     serve(s2, 3)
     serve(s3, 2)
+    block(1, 0)
     serve(s5, 1)
-    compute_right(1)
-    compute_left(1)
+    block(1, 1)
+    block(0, 1)
     serve(s4, 2)
     lax.fori_loop(1, 8, await_masks, 0)
     lmask = jnp.concatenate([lm[k] for k in range(8)], axis=1)

time: 84.8 us -> 84.4 us (level); the launches traced: 84.7 us -> 83 us
  Pallas kernels: 81.5 us -> 79.8 us
    pallas_call x1, Pallas kernels: 81.5 us -> 79.8 us  [shards(): pl.pallas_call(kernel, out_shape=jax.ShapeDtypeStruct((64, 128, DEPTH), B...]
where the time goes in v6:
time: 84.4 us; the launch traced here: 83 us
  Pallas kernels  79.8 us (95%)
  local copies, waits for them, and re-layouts  3.16 us (4%)
    pallas_call x1, Pallas kernels, shards(): pl.pallas_call(kernel, out_shape=jax.ShapeDtypeStruct((64, 128, DEPTH), B...  79.8 us
    unnamed x1, local copies, waits for them, and re-layouts  3.16 us

profile of v6, /device:TPU:1, one launch (start us, length us, event | category | flops | bytes accessed | tf_op | source)
XLA Modules:
  0.0 83.0 jit_solution(12700406261034067881)
XLA Ops:
  0.0 79.8 %shard_map.100 = bf16[64,128,128]{2,1,0:T(8,128)(2,1)} custom-call(bf16[8,1024,256]{2,1,0:T(8,128)(2,1)} %x_hbm.1, s32[8,1024]{1,0:T(8,128)} %m_ref.1, f32[1,256]{1,0:T(1,128)} %bitcast.9, f32[1,256]{1,0:T(1,128)} %bitcast.10, bf16[32,256]{1,0:T(8,128)(2,1)} %bitcast.7, f32[1,32]{1,0:T(1,128)} %bitcast.11, bf16[32,256]{1,0:T(8,128)(2,1)} %bitcast.8, ...), custom_call_target="tpu_custom_call" | custom-call | flops 20000000000 | bytes 8000000 | tf_op jit(solution)/shard_map/pallas_call | solution.py:418
  79.8 3.2 %copy.12 = bf16[64,128,128]{2,1,0:T(8,128)(2,1)} copy(bf16[64,128,128]{2,1,0:T(8,128)(2,1)} %shard_map.100) | data formatting | bytes 4194304
